TPU v7x, 32 devices: a whole 2x2x4 slice. The times are simulated.
32 devices in a mesh: cin: 8 (over z, x), cout: 2 (over y), depth: 2 (over core).
Axes of the slice: x: 2, y: 2, z: 4, core: 2. Of those that a mesh axis runs over, the one named last changes fastest.
Arguments:
- features: bfloat16 [8, 512, 4, 128], P(None, 'cin', 'depth'), may hold values from -6 to 6
- kernel: bfloat16 [27, 512, 512], P(None, 'cout', 'cin'), may hold values from -0.0546875 to 0.0546875
- grad_out: bfloat16 [8, 512, 4, 128], P('cin', 'cout', 'depth'), may hold values from -6 to 6
Outputs:
- output: bfloat16 [8, 512, 4, 128], P('cin', 'cout', 'depth')
- input_grad: bfloat16 [8, 512, 4, 128], P('cout', 'cin', 'depth')
- kernel_grad: float32 [27, 512, 512], P(None, 'cout', 'cin')
All inputs are finite; a program needn't handle non-finite values.
Results may differ from a plain program's by a relative error of at most 0.001.
Values may be sent and summed in bfloat16 or wider, within the bound.
No kernel may reach another device: no remote copies, remote signals or barrier semaphores. Data moves between devices by JAX's collectives and lax.ppermute only.
A program may use at most 128 MiB of HBM per device.

v0:
```python
import math
import jax
import jax.numpy as jnp
from jax import lax
from jax.sharding import PartitionSpec as P


def padded_2(x, sides, width):
    for axis, dim in sides:
        size, length = (lax.axis_size(axis), x.shape[dim])
        up = [(i, (i + 1) % size) for i in range(size - 1)]
        down = [(j, i) for i, j in up]
        last = lax.slice_in_dim(x, length - width, length, axis=dim)
        first = lax.slice_in_dim(x, 0, width, axis=dim)
        before = lax.ppermute(last, axis, up)
        after = lax.ppermute(first, axis, down)
        x = jnp.concatenate([before, x, after], axis=dim)
    return x


def conv_rows(padded, weight, count, slab, width):
    total = None
    for depth_off in range(3):
        pieces = [
            padded[
                row_off : row_off + count,
                :,
                depth_off : depth_off + slab,
                col_off : col_off + width,
            ]
            for row_off in range(3)
            for col_off in range(3)
        ]
        stacked = jnp.stack(pieces, axis=1)
        term = jnp.einsum(
            "toc,htcdw->hodw",
            weight[9 * depth_off : 9 * depth_off + 9],
            stacked,
            preferred_element_type=jnp.float32,
        )
        total = term if total is None else total + term
    return total


def weight_terms(padded, grad_own, count, slab, width):
    parts = []
    for depth_off in range(3):
        pieces = [
            padded[
                row_off : row_off + count,
                :,
                depth_off : depth_off + slab,
                col_off : col_off + width,
            ]
            for row_off in range(3)
            for col_off in range(3)
        ]
        stacked = jnp.stack(pieces, axis=1)
        parts.append(
            jnp.einsum("hodw,htcdw->toc", grad_own, stacked, preferred_element_type=jnp.float32)
        )
    return jnp.concatenate(parts, axis=0)


def per_device(features, kernel, grad_out):
    rows_all = features.shape[0]
    slab = features.shape[2]
    width = features.shape[3]
    chan_in = features.shape[1]
    rows_own = rows_all // lax.axis_size("cin")
    slab_ext = padded_2(features, (("depth", 2),), 1)
    feat_pad = jnp.pad(slab_ext, ((1, 1), (0, 0), (0, 0), (1, 1)))
    block = feat_pad
    output = lax.psum_scatter(
        conv_rows(block, kernel, lax.axis_size("cin") * rows_own, slab, width),
        "cin",
        scatter_dimension=0,
        tiled=True,
    ).astype(jnp.bfloat16)
    grad_full = lax.all_gather(grad_out, "cin", axis=0, tiled=True)
    grad_full = padded_2(grad_full, (("depth", 2),), 1)
    grad_pad = jnp.pad(grad_full, ((1, 1), (0, 0), (0, 0), (0, 0)))
    rows_grad = rows_all // lax.axis_size("cout")
    block = grad_pad
    total = jnp.zeros((lax.axis_size("cout") * rows_grad, chan_in, slab, width), jnp.float32)
    for depth_off in range(3):
        part = block[:, :, 2 - depth_off : 2 - depth_off + slab, :]
        mixed = jnp.einsum(
            "toc,hodw->thcdw",
            kernel[9 * depth_off : 9 * depth_off + 9],
            part,
            preferred_element_type=jnp.float32,
        )
        mixed = jnp.pad(mixed, ((0, 0), (0, 0), (0, 0), (0, 0), (1, 1)))
        for row_off in range(3):
            for col_off in range(3):
                total = (
                    total
                    + mixed[
                        3 * row_off + col_off,
                        2 - row_off : 2 - row_off + lax.axis_size("cout") * rows_grad,
                        :,
                        :,
                        2 - col_off : 2 - col_off + width,
                    ]
                )
    input_grad = lax.psum_scatter(total, "cout", scatter_dimension=0, tiled=True).astype(
        jnp.bfloat16
    )
    grad_own = grad_full[:, :, 1 : 1 + slab, :]
    local_terms = weight_terms(feat_pad, grad_own, rows_all, slab, width)
    summed = lax.psum(local_terms, "depth")
    cells = rows_all * slab * lax.axis_size("depth") * width
    kernel_grad = summed * (1.0 / math.sqrt(cells))
    return (output, input_grad, kernel_grad)


def solution(mesh):
    return jax.shard_map(
        per_device,
        mesh=mesh,
        in_specs=(
            P(None, "cin", "depth", None),
            P(None, "cout", "cin"),
            P("cin", "cout", "depth", None),
        ),
        out_specs=(
            P("cin", "cout", "depth", None),
            P("cout", "cin", "depth", None),
            P(None, "cout", "cin"),
        ),
        check_vma=False,
    )
```

profile of v0, /device:TPU:0, one launch (start us, length us, event | category | flops | bytes accessed | tf_op | source)
XLA Modules:
  0.0 189.4 jit_solution(8112478354780090528)
XLA Ops:
  7.2 0.0 all-gather.2.cloned.1.call-start
  7.2 1.0 copy.40
  8.2 2.4 %collective-permute-start = (bf16[8,64,1,128]{3,1,2,0:T(8,128)(2,1)S(1)}, bf16[8,64,1,128]{3,1,2,0:T(8,128)(2,1)S(1)}, u32[]{:S(2)}, u32[]{:S(2)}) collective-permute-start(bf16[8,64,1,128]{3,1,2,0:T(8,128)(2,1)S(1)} %get-tuple-element.25), channel_id=1, source_target_pairs={{0,1},{2,3},{4,5},{6,7},{8,9},{10,11},{12,13},{14,15},{16,17},{18,... | collective-permute-start | bytes 393224 | tf_op jit(solution)/shard_map/ppermute | solution.py:15
  10.6 1.3 collective-permute-start.1
  11.9 1.6 copy.55
  13.5 0.0 all-gather.2.cloned.1.call-update
  13.5 0.0 reduce-scatter.5.cloned.1.call-start
  13.6 0.0 collective-permute-done
  13.6 0.3 collective-permute-done.1
  13.9 0.5 select_maximum_fusion
  14.4 0.7 fusion.85
  15.1 0.8 fusion.95
  15.9 0.9 fusion.94
  16.8 0.9 fusion.93
  17.6 0.8 fusion.92
  18.4 0.9 fusion.84
  19.3 1.0 fusion.83
  20.3 0.9 fusion.82
  21.2 0.8 fusion.91
  22.0 0.0 copy-done.2
  22.0 0.8 bitcast_dynamic-update-slice_fusion
  22.8 0.9 fusion.81
  23.7 0.7 fusion.73
  24.4 0.9 fusion.89
  25.2 0.8 fusion.88
  26.0 0.8 fusion.87
  26.9 0.9 fusion.80
  27.8 0.9 fusion.79
  28.7 28.0 %all-gather.2.cloned.1.call-done = bf16[8,256,2,128]{3,1,2,0:T(8,128)(2,1)} async-done(((bf16[1,256,2,128]{3,1,2,0:T(8,128)(2,1)}), bf16[8,256,2,128]{3,1,2,0:T(8,128)(2,1)}) %all-gather.2.cloned.1.call-update) | async-done | bytes 1048592 | tf_op jit(solution)/shard_map/all_gather | solution.py:80
  56.7 1.4 fusion.104
  58.0 1.3 collective-permute-start.2
  59.4 1.3 collective-permute-start.3
  60.7 0.9 fusion.86
  61.6 1.0 fusion.78
  62.6 0.8 fusion.68
  63.4 0.0 collective-permute-done.2
  63.4 0.0 collective-permute-done.3
  63.4 0.0 copy-done
  63.5 0.4 fusion.5
  63.8 0.8 copy-done.1
  64.6 0.9 convolution_bitcast_fusion.1
  65.5 0.9 convolution_bitcast_fusion.2
  66.5 0.9 convolution_bitcast_fusion
  67.4 3.3 %fusion.54 = f32[8,64,2,128]{3,1,2,0:T(8,128)} fusion(f32[9,10,64,2,128]{4,2,3,1,0:T(8,128)S(1)} %convolution_bitcast_fusion, f32[9,10,64,2,128]{4,2,3,1,0:T(8,128)S(1)} %convolution_bitcast_fusion.1, f32[9,10,64,2,128]{4,2,0,3,1:T(8,128)S(1)} %convolution_bitcast_fusion.2), kind=kLoop, calls=%fused_computation.90 | loop fusion | flops 3407872 | bytes 22937600 | tf_op jit(solution)/shard_map/add | solution.py:98
  70.7 0.0 reduce-scatter.5.cloned.1.call-update
  70.8 0.0 all-reduce.7.cloned.1.call-start
  70.8 2.5 %convolution_bitcast_fusion.3 = f32[9,256,64]{1,2,0:T(8,128)S(1)} fusion(bf16[8,9,64,2,128]{4,2,3,0,1:T(8,128)(2,1)} %fusion.68, bf16[8,256,2,128]{3,1,2,0:T(8,128)(2,1)S(1)} %copy-done), kind=kOutput, calls=%fused_computation.55 | convolution fusion | flops 603979776 | bytes 3997696 | tf_op jit(solution)/shard_map/hodw,htcdw->toc/dot_general | solution.py:60
  73.3 2.5 %convolution_bitcast_fusion.4 = f32[9,256,64]{1,2,0:T(8,128)S(1)} fusion(bf16[8,9,64,2,128]{4,2,3,0,1:T(8,128)(2,1)} %get-tuple-element.9, bf16[8,256,2,128]{3,1,2,0:T(8,128)(2,1)S(1)} %copy-done), kind=kOutput, calls=%fused_computation.56 | convolution fusion | flops 603979776 | bytes 3997696 | tf_op jit(solution)/shard_map/hodw,htcdw->toc/dot_general | solution.py:60
  75.8 2.6 %fusion.19 = f32[9,256,64]{1,2,0:T(8,128)S(1)} fusion(bf16[8,9,64,2,128]{4,2,1,3,0:T(8,128)(2,1)} %fusion.86, bf16[8,256,2,128]{3,1,2,0:T(8,128)(2,1)S(1)} %copy-done), kind=kOutput, calls=%fused_computation.54 | convolution fusion | flops 603979776 | bytes 3997696 | tf_op jit(solution)/shard_map/hodw,htcdw->toc/dot_general | solution.py:60
  78.3 1.4 pad_maximum_fusion
  79.7 0.0 all-reduce.7.cloned.1.call-update
  79.7 0.2 reduce-scatter.3.cloned.1.call-start
  80.0 2.7 %fusion.13 = f32[8,2,128,256,1]{3,2,0,1,4:T(8,128)S(1)} fusion(bf16[8,9,64,2,128]{4,2,3,0,1:T(8,128)(2,1)} %get-tuple-element.9, bf16[27,256,64]{1,2,0:T(8,128)(2,1)S(1)} %copy-done.1), kind=kOutput, calls=%fused_computation.40 | convolution fusion | flops 603979776 | bytes 4751360 | tf_op jit(solution)/shard_map/toc,htcdw->hodw/dot_general | solution.py:35
  82.7 2.7 %fusion.11 = f32[8,2,128,256,1]{3,2,0,1,4:T(8,128)S(1)} fusion(bf16[8,9,64,2,128]{4,2,3,0,1:T(8,128)(2,1)} %fusion.68, bf16[27,256,64]{1,2,0:T(8,128)(2,1)S(1)} %copy-done.1), kind=kOutput, calls=%fused_computation.38 | convolution fusion | flops 603979776 | bytes 4751360 | tf_op jit(solution)/shard_map/toc,htcdw->hodw/dot_general | solution.py:35
  85.5 4.1 %fusion.15 = f32[8,256,2,128]{1,3,2,0:T(8,128)} fusion(f32[8,2,128,256,1]{3,2,0,1,4:T(8,128)S(1)} %fusion.11, f32[8,2,128,256,1]{3,2,0,1,4:T(8,128)S(1)} %fusion.13, bf16[8,9,64,2,128]{4,2,1,3,0:T(8,128)(2,1)} %fusion.86, bf16[27,256,64]{1,2,0:T(8,128)(2,1)S(1)} %copy-done.1), kind=kOutput, calls=%fused_computation.43 | convolution fusion | flops 605028352 | bytes 8945664 | tf_op jit(solution)/shard_map/toc,htcdw->hodw/dot_general | solution.py:35
  89.5 0.0 reduce-scatter.3.cloned.1.call-update
  89.6 0.0 reduce-scatter.5.cloned.1.call-done
  89.6 1.0 convert_element_type.15
  90.6 0.8 copy.73
  91.4 17.4 %all-reduce.7.cloned.1.call-done = f32[27,256,64]{1,2,0:T(8,128)} async-done(((f32[27,256,64]{1,2,0:T(8,128)}), f32[27,256,64]{1,2,0:T(8,128)}) %all-reduce.7.cloned.1.call-update) | async-done | bytes 1769488 | tf_op jit(solution)/shard_map/psum | solution.py:112
  108.8 2.9 %broadcast_multiply_fusion = f32[27,256,64]{1,2,0:T(8,128)} fusion(f32[27,256,64]{1,2,0:T(8,128)} %all-reduce.7.cloned.1.call-done), kind=kLoop, calls=%fused_computation.58 | loop fusion | flops 442368 | bytes 3538944 | tf_op jit(solution)/shard_map/mul | solution.py:114
  111.7 69.4 %reduce-scatter.3.cloned.1.call-done = f32[1,256,2,128]{1,3,2,0:T(8,128)} async-done(((f32[8,256,2,128]{1,3,2,0:T(8,128)}), f32[1,256,2,128]{1,3,2,0:T(8,128)}) %reduce-scatter.3.cloned.1.call-update) | async-done | bytes 262160 | tf_op jit(solution)/shard_map/reduce_scatter | solution.py:74
  181.1 1.0 convert_element_type.14
  182.1 0.8 copy.72
  (4 shorter events, 0.0 us)
Async XLA Ops:
  7.2 49.5 %all-gather.2.cloned.1.call-start = ((), (), s32[]{:S(2)}) async-start(), calls=%async_computation.3 | async-start | bytes 1179648 | tf_op jit(solution)/shard_map/all_gather | solution.py:80
  8.2 5.3 %collective-permute-start = (bf16[8,64,1,128]{3,1,2,0:T(8,128)(2,1)S(1)}, bf16[8,64,1,128]{3,1,2,0:T(8,128)(2,1)S(1)}, u32[]{:S(2)}, u32[]{:S(2)}) collective-permute-start(bf16[8,64,1,128]{3,1,2,0:T(8,128)(2,1)S(1)} %get-tuple-element.25), channel_id=1, source_target_pairs={{0,1},{2,3},{4,5},{6,7},{8,9},{10,11},{12,13},{14,15},{16,17},{18,... | collective-permute-start | bytes 393224 | tf_op jit(solution)/shard_map/ppermute | solution.py:15
  10.6 3.2 %collective-permute-start.1 = (bf16[8,64,1,128]{3,1,2,0:T(8,128)(2,1)S(1)}, bf16[8,64,1,128]{3,1,2,0:T(8,128)(2,1)S(1)}, u32[]{:S(2)}, u32[]{:S(2)}) collective-permute-start(bf16[8,64,1,128]{3,1,2,0:T(8,128)(2,1)S(1)} %get-tuple-element.26), channel_id=1, source_target_pairs={{1,0},{3,2},{5,4},{7,6},{9,8},{11,10},{13,12},{15,14},{17,16},{19,... | collective-permute-start | bytes 393224 | tf_op jit(solution)/shard_map/ppermute | solution.py:16
  13.5 76.1 %reduce-scatter.5.cloned.1.call-start = ((), (), s32[]{:S(2)}) async-start(), calls=%async_computation.4 | async-start | bytes 786432 | tf_op jit(solution)/shard_map/reduce_scatter | solution.py:107
  16.8 5.2 %copy-start.2 = (bf16[8,64,2,128]{3,2,1,0:T(2,128)(2,1)S(1)}, bf16[8,64,2,128]{3,2,1,0:T(2,128)(2,1)}, u32[]{:S(2)}) copy-start(bf16[8,64,2,128]{3,2,1,0:T(2,128)(2,1)} %param.3) | copy-start | bytes 786436
  56.7 6.8 %copy-start = (bf16[8,256,2,128]{3,1,2,0:T(8,128)(2,1)S(1)}, bf16[8,256,2,128]{3,1,2,0:T(8,128)(2,1)}, u32[]{:S(2)}) copy-start(bf16[8,256,2,128]{3,1,2,0:T(8,128)(2,1)} %all-gather.2.cloned.1.call-done) | copy-start | bytes 3145732
  58.0 5.4 %collective-permute-start.2 = (bf16[8,256,1,128]{3,1,2,0:T(8,128)(2,1)S(1)}, bf16[8,256,1,128]{3,1,2,0:T(8,128)(2,1)S(1)}, u32[]{:S(2)}, u32[]{:S(2)}) collective-permute-start(bf16[8,256,1,128]{3,1,2,0:T(8,128)(2,1)S(1)} %get-tuple-element.23), channel_id=1, source_target_pairs={{0,1},{2,3},{4,5},{6,7},{8,9},{10,11},{12,13},{14,15},{16,17},{18,... | collective-permute-start | bytes 1572872 | tf_op jit(solution)/shard_map/ppermute | solution.py:15
  59.4 4.1 %collective-permute-start.3 = (bf16[8,256,1,128]{3,1,2,0:T(8,128)(2,1)S(1)}, bf16[8,256,1,128]{3,1,2,0:T(8,128)(2,1)S(1)}, u32[]{:S(2)}, u32[]{:S(2)}) collective-permute-start(bf16[8,256,1,128]{3,1,2,0:T(8,128)(2,1)S(1)} %get-tuple-element.24), channel_id=1, source_target_pairs={{1,0},{3,2},{5,4},{7,6},{9,8},{11,10},{13,12},{15,14},{17,16},{19,... | collective-permute-start | bytes 1572872 | tf_op jit(solution)/shard_map/ppermute | solution.py:16
  63.4 1.2 copy-start.1
  70.8 38.1 %all-reduce.7.cloned.1.call-start = ((), (), s32[]{:S(2)}) async-start(), calls=%async_computation.5 | async-start | bytes 3538944 | tf_op jit(solution)/shard_map/psum | solution.py:112
  79.7 101.4 %reduce-scatter.3.cloned.1.call-start = ((), (), s32[]{:S(2)}) async-start(), calls=%async_computation.2 | async-start | bytes 2359296 | tf_op jit(solution)/shard_map/reduce_scatter | solution.py:74
Sparse Core Ops, SparseCore 0:
  13.6 42.9 all-gather.1
  70.9 14.0 reduce-scatter.4
  88.1 20.6 all-reduce.6
  112.2 68.8 reduce-scatter.2
where the time goes:
time: 190 us; the launch traced here: 189 us
  waiting for transfers between devices  115 us (61%)
  local copies, waits for them, and re-layouts  21.9 us (12%)
  matrix products  19.9 us (10%)
  between operations  13.9 us (7%)
  other arithmetic  11.9 us (6%)
  starting transfers between devices  6.61 us (3%)
    reduce_scatter x1, waiting for transfers between devices, per_device(): lax.psum_scatter(conv_rows(block, kernel, lax.axis_size('cin') * rows_own...  69.4 us
    all_gather x1, waiting for transfers between devices, per_device(): grad_full = lax.all_gather(grad_out, 'cin', axis=0, tiled=True)  28 us
    unnamed x25, local copies, waits for them, and re-layouts  17.7 us
    psum x1, waiting for transfers between devices, per_device(): summed = lax.psum(local_terms, 'depth')  17.4 us
    dot_general x3, matrix products, conv_rows(): jnp.einsum('toc,htcdw->hodw', weight[9 * depth_off:9 * depth_off + 9], st...  9.56 us
    dot_general x3, matrix products, weight_terms(): jnp.einsum('hodw,htcdw->toc', grad_own, stacked, preferred_element_type=j...  7.5 us
  transfers between devices with their start and end apart: 8, of which 4 were waited for; matrix products, arithmetic and copies ran while one was open for 22% of the time, Pallas kernels for 0%

commit v1 on v0

--- a/solution.py
+++ b/solution.py
@@ -77,7 +77,24 @@
         scatter_dimension=0,
         tiled=True,
     ).astype(jnp.bfloat16)
-    grad_full = lax.all_gather(grad_out, "cin", axis=0, tiled=True)
+    count_2, here, rows = (lax.axis_size("cin"), lax.axis_index("cin"), grad_out.shape[0])
+    right = [(i_2, (i_2 + 1) % count_2) for i_2 in range(count_2)]
+    left = [(i_2, (i_2 - 1) % count_2) for i_2 in range(count_2)]
+    out = jnp.zeros((*grad_out.shape[:0], count_2 * rows, *grad_out.shape[0 + 1 :]), grad_out.dtype)
+    out = lax.dynamic_update_slice_in_dim(out, grad_out, here * rows, axis=0)
+    from_left = from_right = grad_out
+    half = count_2 // 2
+    for step in range(1, half + 1):
+        from_left = lax.ppermute(from_left, "cin", right)
+        out = lax.dynamic_update_slice_in_dim(
+            out, from_left, (here - step) % count_2 * rows, axis=0
+        )
+        if step < count_2 - half:
+            from_right = lax.ppermute(from_right, "cin", left)
+            out = lax.dynamic_update_slice_in_dim(
+                out, from_right, (here + step) % count_2 * rows, axis=0
+            )
+    grad_full = out
     grad_full = padded_2(grad_full, (("depth", 2),), 1)
     grad_pad = jnp.pad(grad_full, ((1, 1), (0, 0), (0, 0), (0, 0)))
     rows_grad = rows_all // lax.axis_size("cout")

time: 190 us -> 155 us (0.82)
  waiting for transfers between devices: 115 us -> 79.4 us
  starting transfers between devices: 6.61 us -> 22.2 us
  matrix products: 19.9 us -> 11.4 us
  local copies, waits for them, and re-layouts: 21.9 us -> 14.6 us
  between operations: 13.9 us -> 16 us
    all_gather x1 -> x0, waiting for transfers between devices: 28 us -> none  [per_device(): grad_full = lax.all_gather(grad_out, 'cin', axis=0, tiled=True)]
    ppermute x0 -> x7, starting transfers between devices: none -> 15.6 us  [the longest x3 9.39 us: per_device(): from_right = lax.ppermute(from_right, 'cin', left)]
    reduce_scatter x1, waiting for transfers between devices: 69.4 us -> 56.2 us  [per_device(): lax.psum_scatter(conv_rows(block, kernel, lax.axis_size('cin') * rows_own...]
    ppermute x0 -> x7, waiting for transfers between devices: none -> 12.6 us  [the longest x4 12.3 us: per_device(): from_left = lax.ppermute(from_left, 'cin', right)]
    psum x1, waiting for transfers between devices: 17.4 us -> 10.4 us  [per_device(): summed = lax.psum(local_terms, 'depth')]
    unnamed x25 -> x43, local copies, waits for them, and re-layouts: 17.7 us -> 11.6 us
    dot_general x3, matrix products: 9.56 us -> 4.54 us  [conv_rows(): jnp.einsum('toc,htcdw->hodw', weight[9 * depth_off:9 * depth_off + 9], st...]
    dot_general x3, matrix products: 7.5 us -> 4.08 us  [weight_terms(): jnp.einsum('hodw,htcdw->toc', grad_own, stacked, preferred_element_type=j...]
  transfers between devices with their start and end apart: 8 -> 14, of which waited for: 4 -> 8; matrix products, arithmetic and copies ran while one was open for 22% -> 15% of each run, Pallas kernels for 0% -> 0%
where the time goes in v1:
time: 155 us; the launch traced here: 154 us
  waiting for transfers between devices  79.4 us (51%)
  starting transfers between devices  22.2 us (14%)
  between operations  16 us (10%)
  local copies, waits for them, and re-layouts  14.6 us (9%)
  matrix products  11.4 us (7%)
  other arithmetic  10.4 us (7%)
    reduce_scatter x1, waiting for transfers between devices, per_device(): lax.psum_scatter(conv_rows(block, kernel, lax.axis_size('cin') * rows_own...  56.2 us
    ppermute x4, waiting for transfers between devices, per_device(): from_left = lax.ppermute(from_left, 'cin', right)  12.3 us
    unnamed x43, local copies, waits for them, and re-layouts  11.6 us
    psum x1, waiting for transfers between devices, per_device(): summed = lax.psum(local_terms, 'depth')  10.4 us
    ppermute x3, starting transfers between devices, per_device(): from_right = lax.ppermute(from_right, 'cin', left)  9.39 us
    ppermute x4, starting transfers between devices, per_device(): from_left = lax.ppermute(from_left, 'cin', right)  6.24 us
    dot_general x3, matrix products, conv_rows(): jnp.einsum('toc,htcdw->hodw', weight[9 * depth_off:9 * depth_off + 9], st...  4.54 us
    dot_general x3, matrix products, weight_terms(): jnp.einsum('hodw,htcdw->toc', grad_own, stacked, preferred_element_type=j...  4.08 us
  transfers between devices with their start and end apart: 14, of which 8 were waited for; matrix products, arithmetic and copies ran while one was open for 15% of the time, Pallas kernels for 0%

profile of v1, /device:TPU:0, one launch (start us, length us, event | category | flops | bytes accessed | tf_op | source)
XLA Modules:
  0.0 154.0 jit_solution(16493737149580959628)
XLA Ops:
  8.0 1.0 copy.6
  9.1 2.4 %collective-permute-start = (bf16[8,64,1,128]{3,1,2,0:T(8,128)(2,1)S(1)}, bf16[8,64,1,128]{3,1,2,0:T(8,128)(2,1)S(1)}, u32[]{:S(2)}, u32[]{:S(2)}) collective-permute-start(bf16[8,64,1,128]{3,1,2,0:T(8,128)(2,1)S(1)} %get-tuple-element.22), channel_id=1, source_target_pairs={{0,1},{2,3},{4,5},{6,7},{8,9},{10,11},{12,13},{14,15},{16,17},{18,... | collective-permute-start | bytes 393224 | tf_op jit(solution)/shard_map/ppermute | solution.py:15
  11.5 1.3 collective-permute-start.1
  12.8 0.2 broadcast_in_dim.3
  13.0 1.6 %fusion.106 = (bf16[1,256,2,128]{3,1,2,0:T(8,128)(2,1)}, bf16[8,256,2,128]{3,1,2,0:T(8,128)(2,1)S(1)}) fusion(bf16[1,256,2,128]{3,2,1,0:T(2,128)(2,1)} %param.5, bf16[8,256,2,128]{3,1,2,0:T(8,128)(2,1)S(1)} %broadcast_in_dim.3, s32[]{:T(128)S(6)} %select_n.55), kind=kLoop, calls=%fused_computation.183 | loop fusion | bytes 393220 | tf_op args[2]
  14.6 2.3 %collective-permute-start.2 = (bf16[1,256,2,128]{3,1,2,0:T(8,128)(2,1)}, bf16[1,256,2,128]{3,1,2,0:T(8,128)(2,1)}, u32[]{:S(2)}, u32[]{:S(2)}) collective-permute-start(bf16[1,256,2,128]{3,1,2,0:T(8,128)(2,1)} %get-tuple-element.24), channel_id=1, source_target_pairs={{0,4},{4,8},{8,12},{12,16},{16,20},{20,24},{24,28},{28,0},{1,5},{5... | collective-permute-start | bytes 393224 | tf_op jit(solution)/shard_map/ppermute | solution.py:88
  16.9 3.0 %collective-permute-start.3 = (bf16[1,256,2,128]{3,1,2,0:T(8,128)(2,1)}, bf16[1,256,2,128]{3,1,2,0:T(8,128)(2,1)}, u32[]{:S(2)}, u32[]{:S(2)}) collective-permute-start(bf16[1,256,2,128]{3,1,2,0:T(8,128)(2,1)} %get-tuple-element.24), channel_id=1, source_target_pairs={{0,28},{4,0},{8,4},{12,8},{16,12},{20,16},{24,20},{28,24},{1,29},{... | collective-permute-start | bytes 393224 | tf_op jit(solution)/shard_map/ppermute | solution.py:93
  20.0 0.6 copy-done.10
  20.6 0.5 select_maximum_fusion
  21.3 0.2 fusion.94
  21.5 0.2 fusion.93
  21.8 0.3 copy-done.6
  22.2 0.2 fusion.89
  22.4 0.2 fusion.84
  22.6 0.4 fusion.83
  23.0 0.2 fusion.82
  23.2 0.1 bitcast_dynamic-update-slice_fusion
  23.3 0.3 fusion.81
  23.6 0.2 fusion.80
  23.9 0.2 fusion.79
  24.1 0.1 fusion.88
  24.2 0.2 collective-permute-done.2
  24.4 1.9 %collective-permute-start.4 = (bf16[1,256,2,128]{3,1,2,0:T(8,128)(2,1)}, bf16[1,256,2,128]{3,1,2,0:T(8,128)(2,1)S(1)}, u32[]{:S(2)}, u32[]{:S(2)}) collective-permute-start(bf16[1,256,2,128]{3,1,2,0:T(8,128)(2,1)} %collective-permute-done.2), channel_id=1, source_target_pairs={{0,4},{4,8},{8,12},{12,16},{16,20},{20,24},{24,28},{28,0},{1,5},{5... | collective-permute-start | bytes 393224 | tf_op jit(solution)/shard_map/ppermute | solution.py:88
  26.2 0.2 fusion.87
  26.5 2.9 %collective-permute-start.5 = (bf16[1,256,2,128]{3,1,2,0:T(8,128)(2,1)}, bf16[1,256,2,128]{3,1,2,0:T(8,128)(2,1)S(1)}, u32[]{:S(2)}, u32[]{:S(2)}) collective-permute-start(bf16[1,256,2,128]{3,1,2,0:T(8,128)(2,1)} %collective-permute-done.3), channel_id=1, source_target_pairs={{0,28},{4,0},{8,4},{12,8},{16,12},{20,16},{24,20},{28,24},{1,29},{... | collective-permute-start | bytes 393224 | tf_op jit(solution)/shard_map/ppermute | solution.py:93
  29.3 0.9 constant_dynamic-update-slice_fusion.6
  30.3 0.9 constant_dynamic-update-slice_fusion.5
  31.2 2.3 %collective-permute-done.4 = bf16[1,256,2,128]{3,1,2,0:T(8,128)(2,1)S(1)} collective-permute-done((bf16[1,256,2,128]{3,1,2,0:T(8,128)(2,1)}, bf16[1,256,2,128]{3,1,2,0:T(8,128)(2,1)S(1)}, u32[]{:S(2)}, u32[]{:S(2)}) %collective-permute-start.4) | collective-permute-done | bytes 131104 | tf_op jit(solution)/shard_map/ppermute | solution.py:88
  33.5 1.3 collective-permute-start.6
  34.8 3.5 %collective-permute-start.7 = (bf16[1,256,2,128]{3,1,2,0:T(8,128)(2,1)S(1)}, bf16[1,256,2,128]{3,1,2,0:T(8,128)(2,1)S(1)}, u32[]{:S(2)}, u32[]{:S(2)}) collective-permute-start(bf16[1,256,2,128]{3,1,2,0:T(8,128)(2,1)S(1)} %collective-permute-done.5), channel_id=1, source_target_pairs={{0,28},{4,0},{8,4},{12,8},{16,12},{20,16},{24,20},{28,24},{1,29},{... | collective-permute-start | bytes 393224 | tf_op jit(solution)/shard_map/ppermute | solution.py:93
  38.3 3.2 %collective-permute-done.6 = bf16[1,256,2,128]{3,1,2,0:T(8,128)(2,1)S(1)} collective-permute-done((bf16[1,256,2,128]{3,1,2,0:T(8,128)(2,1)S(1)}, bf16[1,256,2,128]{3,1,2,0:T(8,128)(2,1)S(1)}, u32[]{:S(2)}, u32[]{:S(2)}) %collective-permute-start.6) | collective-permute-done | bytes 131104 | tf_op jit(solution)/shard_map/ppermute | solution.py:88
  41.5 0.8 collective-permute-start.8
  42.3 0.3 collective-permute-done.7
  42.6 6.6 %collective-permute-done.8 = bf16[1,256,2,128]{3,1,2,0:T(8,128)(2,1)S(1)} collective-permute-done((bf16[1,256,2,128]{3,1,2,0:T(8,128)(2,1)S(1)}, bf16[1,256,2,128]{3,1,2,0:T(8,128)(2,1)S(1)}, u32[]{:S(2)}, u32[]{:S(2)}) %collective-permute-start.8) | collective-permute-done | bytes 131104 | tf_op jit(solution)/shard_map/ppermute | solution.py:88
  49.3 1.3 collective-permute-start.9
  50.6 1.3 collective-permute-start.10
  51.9 0.2 fusion.86
  52.1 0.3 fusion.78
  52.5 0.2 fusion.68
  52.7 1.5 %copy-done = bf16[8,9,64,2,128]{4,2,3,0,1:T(8,128)(2,1)} copy-done((bf16[8,9,64,2,128]{4,2,3,0,1:T(8,128)(2,1)}, bf16[8,9,64,2,128]{4,2,3,0,1:T(8,128)(2,1)S(1)}, u32[]{:S(2)}) %copy-start) | copy-done | bytes 2359320
  54.3 0.2 collective-permute-done.10
  54.4 0.3 fusion.5
  54.8 0.9 convolution_bitcast_fusion.1
  55.7 0.9 convolution_bitcast_fusion.2
  56.7 0.9 convolution_bitcast_fusion
  57.6 3.3 %fusion.54 = f32[8,64,2,128]{3,1,2,0:T(8,128)} fusion(f32[9,10,64,2,128]{4,2,3,1,0:T(8,128)S(1)} %convolution_bitcast_fusion, f32[9,10,64,2,128]{4,2,3,1,0:T(8,128)S(1)} %convolution_bitcast_fusion.1, f32[9,10,64,2,128]{4,2,0,3,1:T(8,128)S(1)} %convolution_bitcast_fusion.2), kind=kLoop, calls=%fused_computation.90 | loop fusion | flops 3407872 | bytes 22937600 | tf_op jit(solution)/shard_map/add | solution.py:115
  60.9 0.2 all-reduce.7.cloned.1.call-start
  61.1 2.5 %convolution_bitcast_fusion.3 = f32[9,256,64]{1,2,0:T(8,128)S(1)} fusion(bf16[8,9,64,2,128]{4,2,3,0,1:T(8,128)(2,1)} %copy-done, bf16[8,256,2,128]{3,1,2,0:T(8,128)(2,1)S(1)} %constant_dynamic-update-slice_fusion), kind=kOutput, calls=%fused_computation.55 | convolution fusion | flops 603979776 | bytes 3997696 | tf_op jit(solution)/shard_map/hodw,htcdw->toc/dot_general | solution.py:60
  63.6 0.8 convolution_bitcast_fusion.4
  64.4 1.0 copy-done.3
  65.4 0.8 fusion.19
  66.3 1.4 pad_maximum_fusion
  67.8 1.0 fusion.13
  68.8 0.6 copy-done.1
  69.4 1.0 fusion.11
  70.5 0.6 copy-done.4
  71.1 2.5 %fusion.15 = f32[8,256,2,128]{1,3,2,0:T(8,128)} fusion(f32[8,2,128,256,1]{3,2,0,1,4:T(8,128)S(1)} %fusion.11, f32[8,2,128,256,1]{3,2,0,1,4:T(8,128)S(1)} %fusion.13, bf16[8,9,64,2,128]{4,2,1,3,0:T(8,128)(2,1)S(1)} %copy-done.4, bf16[27,256,64]{1,2,0:T(8,128)(2,1)S(1)} %copy-done.8), kind=kOutput, calls=%fused_computation.43 | convolution fusion | flops 605028352 | bytes 8945664 | tf_op jit(solution)/shard_map/toc,htcdw->hodw/dot_general | solution.py:35
  73.6 1.0 convert_element_type.15
  74.6 0.8 copy.41
  75.4 10.4 %all-reduce.7.cloned.1.call-done = f32[27,256,64]{1,2,0:T(8,128)} async-done(((f32[27,256,64]{1,2,0:T(8,128)}), f32[27,256,64]{1,2,0:T(8,128)}) %all-reduce.7.cloned.1.call-update) | async-done | bytes 1769488 | tf_op jit(solution)/shard_map/psum | solution.py:129
  85.8 2.9 %broadcast_multiply_fusion = f32[27,256,64]{1,2,0:T(8,128)} fusion(f32[27,256,64]{1,2,0:T(8,128)} %all-reduce.7.cloned.1.call-done), kind=kLoop, calls=%fused_computation.58 | loop fusion | flops 442368 | bytes 3538944 | tf_op jit(solution)/shard_map/mul | solution.py:131
  88.6 56.2 %reduce-scatter.3.cloned.1.call-done = f32[1,256,2,128]{1,3,2,0:T(8,128)} async-done(((f32[8,256,2,128]{1,3,2,0:T(8,128)}), f32[1,256,2,128]{1,3,2,0:T(8,128)}) %reduce-scatter.3.cloned.1.call-update) | async-done | bytes 262160 | tf_op jit(solution)/shard_map/reduce_scatter | solution.py:74
  144.8 1.0 convert_element_type.14
  145.8 0.8 copy.40
  (41 shorter events, 0.7 us)
Async XLA Ops:
  8.0 65.6 %reduce-scatter.5.cloned.1.call-start = ((), (), s32[]{:S(2)}) async-start(), calls=%async_computation.3 | async-start | bytes 786432 | tf_op jit(solution)/shard_map/reduce_scatter | solution.py:124
  9.0 10.9 %copy-start.5 = (bf16[8,64,2,128]{3,1,2,0:T(8,128)(2,1)}, bf16[8,64,2,128]{3,1,2,0:T(8,128)(2,1)S(1)}, u32[]{:S(2)}) copy-start(bf16[8,64,2,128]{3,1,2,0:T(8,128)(2,1)S(1)} %copy.6) | copy-start | bytes 786436
  9.1 10.9 %collective-permute-start = (bf16[8,64,1,128]{3,1,2,0:T(8,128)(2,1)S(1)}, bf16[8,64,1,128]{3,1,2,0:T(8,128)(2,1)S(1)}, u32[]{:S(2)}, u32[]{:S(2)}) collective-permute-start(bf16[8,64,1,128]{3,1,2,0:T(8,128)(2,1)S(1)} %get-tuple-element.22), channel_id=1, source_target_pairs={{0,1},{2,3},{4,5},{6,7},{8,9},{10,11},{12,13},{14,15},{16,17},{18,... | collective-permute-start | bytes 393224 | tf_op jit(solution)/shard_map/ppermute | solution.py:15
  11.5 8.5 %collective-permute-start.1 = (bf16[8,64,1,128]{3,1,2,0:T(8,128)(2,1)S(1)}, bf16[8,64,1,128]{3,1,2,0:T(8,128)(2,1)S(1)}, u32[]{:S(2)}, u32[]{:S(2)}) collective-permute-start(bf16[8,64,1,128]{3,1,2,0:T(8,128)(2,1)S(1)} %get-tuple-element.23), channel_id=1, source_target_pairs={{1,0},{3,2},{5,4},{7,6},{9,8},{11,10},{13,12},{15,14},{17,16},{19,... | collective-permute-start | bytes 393224 | tf_op jit(solution)/shard_map/ppermute | solution.py:16
  14.6 9.8 %collective-permute-start.2 = (bf16[1,256,2,128]{3,1,2,0:T(8,128)(2,1)}, bf16[1,256,2,128]{3,1,2,0:T(8,128)(2,1)}, u32[]{:S(2)}, u32[]{:S(2)}) collective-permute-start(bf16[1,256,2,128]{3,1,2,0:T(8,128)(2,1)} %get-tuple-element.24), channel_id=1, source_target_pairs={{0,4},{4,8},{8,12},{12,16},{16,20},{20,24},{24,28},{28,0},{1,5},{5... | collective-permute-start | bytes 393224 | tf_op jit(solution)/shard_map/ppermute | solution.py:88
  16.9 9.5 %collective-permute-start.3 = (bf16[1,256,2,128]{3,1,2,0:T(8,128)(2,1)}, bf16[1,256,2,128]{3,1,2,0:T(8,128)(2,1)}, u32[]{:S(2)}, u32[]{:S(2)}) collective-permute-start(bf16[1,256,2,128]{3,1,2,0:T(8,128)(2,1)} %get-tuple-element.24), channel_id=1, source_target_pairs={{0,28},{4,0},{8,4},{12,8},{16,12},{20,16},{24,20},{28,24},{1,29},{... | collective-permute-start | bytes 393224 | tf_op jit(solution)/shard_map/ppermute | solution.py:93
  20.0 0.7 copy-start.10
  21.1 1.0 copy-start.6
  21.2 1.0 copy-start.11
  21.7 1.5 %copy-start.9 = (bf16[8,64,2,128]{3,2,1,0:T(2,128)(2,1)S(1)}, bf16[8,64,2,128]{3,2,1,0:T(2,128)(2,1)}, u32[]{:S(2)}) copy-start(bf16[8,64,2,128]{3,2,1,0:T(2,128)(2,1)} %param.3) | copy-start | bytes 786436
  24.4 9.2 %collective-permute-start.4 = (bf16[1,256,2,128]{3,1,2,0:T(8,128)(2,1)}, bf16[1,256,2,128]{3,1,2,0:T(8,128)(2,1)S(1)}, u32[]{:S(2)}, u32[]{:S(2)}) collective-permute-start(bf16[1,256,2,128]{3,1,2,0:T(8,128)(2,1)} %collective-permute-done.2), channel_id=1, source_target_pairs={{0,4},{4,8},{8,12},{12,16},{16,20},{20,24},{24,28},{28,0},{1,5},{5... | collective-permute-start | bytes 393224 | tf_op jit(solution)/shard_map/ppermute | solution.py:88
  26.5 8.3 %collective-permute-start.5 = (bf16[1,256,2,128]{3,1,2,0:T(8,128)(2,1)}, bf16[1,256,2,128]{3,1,2,0:T(8,128)(2,1)S(1)}, u32[]{:S(2)}, u32[]{:S(2)}) collective-permute-start(bf16[1,256,2,128]{3,1,2,0:T(8,128)(2,1)} %collective-permute-done.3), channel_id=1, source_target_pairs={{0,28},{4,0},{8,4},{12,8},{16,12},{20,16},{24,20},{28,24},{1,29},{... | collective-permute-start | bytes 393224 | tf_op jit(solution)/shard_map/ppermute | solution.py:93
  33.5 8.0 %collective-permute-start.6 = (bf16[1,256,2,128]{3,1,2,0:T(8,128)(2,1)S(1)}, bf16[1,256,2,128]{3,1,2,0:T(8,128)(2,1)S(1)}, u32[]{:S(2)}, u32[]{:S(2)}) collective-permute-start(bf16[1,256,2,128]{3,1,2,0:T(8,128)(2,1)S(1)} %collective-permute-done.4), channel_id=1, source_target_pairs={{0,4},{4,8},{8,12},{12,16},{16,20},{20,24},{24,28},{28,0},{1,5},{5... | collective-permute-start | bytes 393224 | tf_op jit(solution)/shard_map/ppermute | solution.py:88
  34.8 7.8 %collective-permute-start.7 = (bf16[1,256,2,128]{3,1,2,0:T(8,128)(2,1)S(1)}, bf16[1,256,2,128]{3,1,2,0:T(8,128)(2,1)S(1)}, u32[]{:S(2)}, u32[]{:S(2)}) collective-permute-start(bf16[1,256,2,128]{3,1,2,0:T(8,128)(2,1)S(1)} %collective-permute-done.5), channel_id=1, source_target_pairs={{0,28},{4,0},{8,4},{12,8},{16,12},{20,16},{24,20},{28,24},{1,29},{... | collective-permute-start | bytes 393224 | tf_op jit(solution)/shard_map/ppermute | solution.py:93
  41.5 7.7 %collective-permute-start.8 = (bf16[1,256,2,128]{3,1,2,0:T(8,128)(2,1)S(1)}, bf16[1,256,2,128]{3,1,2,0:T(8,128)(2,1)S(1)}, u32[]{:S(2)}, u32[]{:S(2)}) collective-permute-start(bf16[1,256,2,128]{3,1,2,0:T(8,128)(2,1)S(1)} %collective-permute-done.6), channel_id=1, source_target_pairs={{0,4},{4,8},{8,12},{12,16},{16,20},{20,24},{24,28},{28,0},{1,5},{5... | collective-permute-start | bytes 393224 | tf_op jit(solution)/shard_map/ppermute | solution.py:88
  49.3 3.4 %collective-permute-start.9 = (bf16[8,256,1,128]{3,1,2,0:T(8,128)(2,1)S(1)}, bf16[8,256,1,128]{3,1,2,0:T(8,128)(2,1)S(1)}, u32[]{:S(2)}, u32[]{:S(2)}) collective-permute-start(bf16[8,256,1,128]{3,1,2,0:T(8,128)(2,1)S(1)} %get-tuple-element.20), channel_id=1, source_target_pairs={{0,1},{2,3},{4,5},{6,7},{8,9},{10,11},{12,13},{14,15},{16,17},{18,... | collective-permute-start | bytes 1572872 | tf_op jit(solution)/shard_map/ppermute | solution.py:15
  50.6 3.8 %collective-permute-start.10 = (bf16[8,256,1,128]{3,1,2,0:T(8,128)(2,1)S(1)}, bf16[8,256,1,128]{3,1,2,0:T(8,128)(2,1)S(1)}, u32[]{:S(2)}, u32[]{:S(2)}) collective-permute-start(bf16[8,256,1,128]{3,1,2,0:T(8,128)(2,1)S(1)} %get-tuple-element.21), channel_id=1, source_target_pairs={{1,0},{3,2},{5,4},{7,6},{9,8},{11,10},{13,12},{15,14},{17,16},{19,... | collective-permute-start | bytes 1572872 | tf_op jit(solution)/shard_map/ppermute | solution.py:16
  52.1 4.5 %copy-start.2 = (bf16[8,9,64,2,128]{4,2,1,3,0:T(8,128)(2,1)}, bf16[8,9,64,2,128]{4,2,1,3,0:T(8,128)(2,1)S(1)}, u32[]{:S(2)}) copy-start(bf16[8,9,64,2,128]{4,2,1,3,0:T(8,128)(2,1)S(1)} %fusion.86) | copy-start | bytes 7077892
  52.7 1.6 %copy-start = (bf16[8,9,64,2,128]{4,2,3,0,1:T(8,128)(2,1)}, bf16[8,9,64,2,128]{4,2,3,0,1:T(8,128)(2,1)S(1)}, u32[]{:S(2)}) copy-start(bf16[8,9,64,2,128]{4,2,3,0,1:T(8,128)(2,1)S(1)} %fusion.68) | copy-start | bytes 7077892
  52.7 2.1 %copy-start.7 = (bf16[27,256,64]{1,2,0:T(8,128)(2,1)S(1)}, bf16[27,256,64]{1,2,0:T(8,128)(2,1)}, u32[]{:S(2)}) copy-start(bf16[27,256,64]{1,2,0:T(8,128)(2,1)} %param.4) | copy-start | bytes 2654212
  60.9 24.9 %all-reduce.7.cloned.1.call-start = ((), (), s32[]{:S(2)}) async-start(), calls=%async_computation.4 | async-start | bytes 3538944 | tf_op jit(solution)/shard_map/psum | solution.py:129
  63.6 1.8 %copy-start.3 = (bf16[8,9,64,2,128]{4,2,1,3,0:T(8,128)(2,1)S(1)}, bf16[8,9,64,2,128]{4,2,1,3,0:T(8,128)(2,1)}, u32[]{:S(2)}) copy-start(bf16[8,9,64,2,128]{4,2,1,3,0:T(8,128)(2,1)} %copy-done.2) | copy-start | bytes 7077892
  66.3 1.5 copy-start.8
  67.7 77.2 %reduce-scatter.3.cloned.1.call-start = ((), (), s32[]{:S(2)}) async-start(), calls=%async_computation.2 | async-start | bytes 2359296 | tf_op jit(solution)/shard_map/reduce_scatter | solution.py:74
  67.8 1.7 %copy-start.1 = (bf16[8,9,64,2,128]{4,2,3,0,1:T(8,128)(2,1)S(1)}, bf16[8,9,64,2,128]{4,2,3,0,1:T(8,128)(2,1)}, u32[]{:S(2)}) copy-start(bf16[8,9,64,2,128]{4,2,3,0,1:T(8,128)(2,1)} %copy-done) | copy-start | bytes 7077892
  69.4 1.7 %copy-start.4 = (bf16[8,9,64,2,128]{4,2,1,3,0:T(8,128)(2,1)S(1)}, bf16[8,9,64,2,128]{4,2,1,3,0:T(8,128)(2,1)}, u32[]{:S(2)}) copy-start(bf16[8,9,64,2,128]{4,2,1,3,0:T(8,128)(2,1)} %copy-done.2) | copy-start | bytes 7077892
Sparse Core Ops, SparseCore 0:
  61.0 12.2 reduce-scatter.4
  77.3 67.5 reduce-scatter.2
Sparse Core Ops, SparseCore 1:
  67.8 17.9 all-reduce.6
